TPU v7x, 32 devices: a whole 2x2x4 slice. The times are simulated.
32 devices in a mesh: slot: 16 (over z, y, core), tp: 2 (over x).
Axes of the slice: x: 2, y: 2, z: 4, core: 2. Of those that a mesh axis runs over, the one named last changes fastest.
Arguments:
- hidden: bfloat16 [7168, 6144], P('slot', 'tp'), may hold values from -4 to 4
- queries: bfloat16 [7168, 3072], P('slot', 'tp'), may hold values from -22 to 22
- key_rows: bfloat16 [7168, 3072], P('slot', 'tp'), may hold values from -6 to 6
- values: bfloat16 [7168, 3072], P('slot', 'tp'), may hold values from -6 to 6
- out_weight: bfloat16 [3072, 6144], P('tp'), may hold values from -0.109375 to 0.109375
- level_table: float32 [64, 6144], P(None, 'tp'), may hold values from 0.3 to 3
- noise_level: int32 [16], P('slot'), may hold values from 0 to 63
- group_live: int32 [16], replicated, may hold values 0 or 1
Outputs:
- refined: bfloat16 [7168, 6144], P('slot', 'tp')
All inputs are finite; a program needn't handle non-finite values.
Results may differ from a plain program's by a relative error of at most 0.014.
Values may be sent and summed in bfloat16 or wider, within the bound.
A program may use at most 192 MiB of HBM per device.

v0:
```python
import math

import jax
import jax.numpy as jnp
from jax import lax
from jax.experimental import pallas as pl
from jax.experimental.pallas import tpu as pltpu
from jax.sharding import PartitionSpec as P

HD = 128
EXP2_SCALE = HD ** (-0.5) * math.log2(math.e)


def passed_along(value, axis, steps):
    count = lax.axis_size(axis)
    pairs = [(source, (source + steps) % count) for source in range(count)]
    return lax.ppermute(value, axis, pairs)


def swapped_with_pair(value):
    count = lax.axis_size("slot")
    return lax.ppermute(value, "slot", [(source, source ^ 1) for source in range(count)])


def attend_kernel(order_ref, count_ref, query_ref, kv_ref, out_ref, top, total, weighted):
    step = pl.program_id(0)
    width = query_ref.shape[1]
    heads = width // HD

    @pl.when(step == 0)
    def _():
        top[...] = jnp.full(top.shape, -1e30, jnp.float32)
        total[...] = jnp.zeros(total.shape, jnp.float32)
        weighted[...] = jnp.zeros(weighted.shape, jnp.float32)

    @pl.when(step < count_ref[0])
    def _():
        for head in range(heads):
            low = head * HD
            scores = lax.dot_general(
                kv_ref[:, low : low + HD],
                query_ref[:, low : low + HD],
                (((1,), (1,)), ((), ())),
                preferred_element_type=jnp.float32,
            )
            old_top = top[head]
            new_top = jnp.maximum(old_top, jnp.max(scores, axis=0, keepdims=True))
            expon = jnp.exp2((scores - new_top) * EXP2_SCALE)
            shrink = jnp.exp2((old_top - new_top) * EXP2_SCALE)
            total[head] = total[head] * shrink + jnp.sum(expon, axis=0, keepdims=True)
            weighted[head] = weighted[head] * shrink + lax.dot_general(
                kv_ref[:, width + low : width + low + HD],
                expon.astype(jnp.bfloat16),
                (((0,), (0,)), ((), ())),
                preferred_element_type=jnp.float32,
            )
            top[head] = new_top

    @pl.when(step == pl.num_programs(0) - 1)
    def _():
        for head in range(heads):
            out_ref[:, head * HD : (head + 1) * HD] = (
                (weighted[head] / total[head]).T.astype(out_ref.dtype)
            )


def attend(order, count, queries, gathered, groups):
    rows, width = queries.shape
    heads = width // HD
    pairs = rows * gathered.shape[0] * heads
    return pl.pallas_call(
        attend_kernel,
        out_shape=jax.ShapeDtypeStruct((rows, width), jnp.bfloat16),
        grid_spec=pltpu.PrefetchScalarGridSpec(
            num_scalar_prefetch=2,
            grid=(groups,),
            in_specs=[
                pl.BlockSpec((rows, width), lambda step, order, count: (0, 0)),
                pl.BlockSpec((rows, 2 * width), lambda step, order, count: (order[step], 0)),
            ],
            out_specs=pl.BlockSpec((rows, width), lambda step, order, count: (0, 0)),
            scratch_shapes=[
                pltpu.VMEM((heads, 1, rows), jnp.float32),
                pltpu.VMEM((heads, 1, rows), jnp.float32),
                pltpu.VMEM((heads, HD, rows), jnp.float32),
            ],
        ),
        compiler_params=pltpu.CompilerParams(vmem_limit_bytes=56 * 1024 * 1024),
        cost_estimate=pl.CostEstimate(
            flops=4 * pairs * HD,
            bytes_accessed=gathered.size * 2 + 4 * rows * width,
            transcendentals=pairs,
        ),
    )(order, count, queries, gathered)


def per_device(hidden, queries, key_rows, values, out_weight, level_table, noise_level, group_live):
    rows, width = queries.shape
    out_width = hidden.shape[1]
    groups = lax.axis_size("slot")
    shards = lax.axis_size("tp")
    own_slot = lax.axis_index("slot")
    own_shard = lax.axis_index("tp")
    group = lax.rem(own_slot + 1, groups)

    heads = width // HD
    cut = (heads - max(1, heads // 4)) * HD

    def gather(low, high, after=None):
        piece = jnp.concatenate([key_rows[:, low:high], values[:, low:high]], axis=1)
        if after is not None:
            piece, after = lax.optimization_barrier((piece, after))
        return lax.all_gather(piece, "slot", axis=0, tiled=True), after

    first, _ = gather(0, cut)
    level = passed_along(noise_level, "slot", -1)
    queries = passed_along(queries, "slot", -1)
    second, (queries, level) = gather(cut, width, (queries, level))

    half = width // 2
    parity = lax.rem(own_slot, 2)
    own_weight = lax.dynamic_slice(out_weight, (0, own_shard * out_width), (width, out_width))
    halves = []
    for shift in range(1, shards):
        target = lax.rem(own_shard + shift, shards)
        sent = lax.dynamic_slice(
            out_weight, (parity * half, target * out_width), (half, out_width)
        )
        halves.append(passed_along(sent, "tp", shift))

    slot_ids = jnp.arange(groups, dtype=jnp.int32)
    needed = ((slot_ids < group) & (group_live == 1)) | (slot_ids == group)
    place = jnp.cumsum(needed.astype(jnp.int32)) - 1
    count = jnp.sum(needed.astype(jnp.int32))
    hits = needed[None, :] & (place[None, :] == slot_ids[:, None])
    order = jnp.where(
        slot_ids < count, jnp.sum(jnp.where(hits, slot_ids[None, :], 0), axis=1), group
    ).astype(jnp.int32)
    count = count.reshape(1)

    def shared(attended):
        others = [passed_along(attended, "tp", shift) for shift in range(1, shards)]
        return jnp.concatenate([attended] + others, axis=1)

    attended = attend(order, count, queries[:, :cut], first, groups)
    attended, queries, halves = lax.optimization_barrier((attended, queries, halves))
    weights = [own_weight]
    for mine in halves:
        other = swapped_with_pair(mine)
        weights += [
            jnp.concatenate(
                [jnp.where(parity == 0, mine, other), jnp.where(parity == 0, other, mine)], axis=0
            )
        ]
    first_weight = jnp.concatenate([weight[:cut] for weight in weights], axis=0)
    second_weight = jnp.concatenate([weight[cut:] for weight in weights], axis=0)
    projected = jnp.dot(shared(attended), first_weight, preferred_element_type=jnp.float32)
    picked = jnp.arange(level_table.shape[0], dtype=jnp.int32) == level[0]
    gate_row = jnp.sum(jnp.where(picked[:, None], level_table, 0.0), axis=0)

    hidden, _ = lax.optimization_barrier((hidden, second[:16, :HD]))
    queries, projected, second_weight = lax.optimization_barrier(
        (queries, projected, second_weight)
    )
    hidden = passed_along(hidden, "slot", -1)
    attended = attend(order, count, queries[:, cut:], second, groups)
    projected = projected + jnp.dot(
        shared(attended), second_weight, preferred_element_type=jnp.float32
    )
    return (hidden.astype(jnp.float32) + gate_row[None, :] * projected).astype(jnp.bfloat16)


def solution(mesh):
    in_specs = (
        P("slot", "tp"),
        P("slot", "tp"),
        P("slot", "tp"),
        P("slot", "tp"),
        P("tp", None),
        P(None, "tp"),
        P("slot"),
        P(),
    )
    out_specs = P("slot", "tp")
    return jax.shard_map(
        per_device, mesh=mesh, in_specs=in_specs, out_specs=out_specs, check_vma=False
    )
```

profile of v0, /device:TPU:25, one launch (start us, length us, event | category | flops | bytes accessed | tf_op | source)
XLA Modules:
  0.0 351.3 jit_solution(87140501073342761)
XLA Ops:
  6.5 1.2 slice-done.2
  7.8 0.3 slice-done.4
  8.1 1.4 pad_maximum_fusion.2
  9.6 0.7 collective-permute-start.1
  10.3 0.8 collective-permute-start.2
  11.2 0.9 pad_maximum_fusion.3
  12.1 32.8 %collective-permute-done.2 = s32[1]{0:T(128)} collective-permute-done((s32[1]{0:T(128)}, s32[1]{0:T(128)}, u32[]{:S(2)}, u32[]{:S(2)}) %collective-permute-start.2) | collective-permute-done | bytes 36 | tf_op jit(solution)/shard_map/ppermute | solution.py:17
  44.9 5.0 %dynamic_slice.6 = bf16[768,3072]{1,0:T(8,128)(2,1)} dynamic-slice(bf16[1536,6144]{1,0:T(8,128)(2,1)} %param.12, s32[]{:T(128)S(6)} %select_n.36, s32[]{:T(128)S(6)} %select_n.37), dynamic_slice_sizes={768,3072} | dynamic-slice | bytes 9437188 | tf_op jit(solution)/shard_map/dynamic_slice | solution.py:126
  49.9 1.2 collective-permute-start.3
  51.1 0.6 convert_reduce_fusion
  52.1 1.1 compare_select_fusion.order_ref
  53.2 2.3 slice.33.query_ref
  55.5 132.1 %all-gather.3.cloned.1.call-done.kv_ref = bf16[7168,2304]{1,0:T(8,128)(2,1)} async-done(((bf16[448,2304]{1,0:T(8,128)(2,1)}), bf16[7168,2304]{1,0:T(8,128)(2,1)}) %all-gather.3.cloned.1.call-update) | async-done | bytes 33030160 | tf_op jit(solution)/shard_map/all_gather | solution.py:113
  187.6 36.2 %shard_map.82 = bf16[448,1152]{1,0:T(8,128)(2,1)} custom-call(s32[16]{0:T(128)} %compare_select_fusion.order_ref, s32[1]{0:T(128)} %bitcast.2.count_ref, bf16[448,1152]{1,0:T(8,128)(2,1)} %slice.33.query_ref, bf16[7168,2304]{1,0:T(8,128)(2,1)} %all-gather.3.cloned.1.call-done.kv_ref), custom_call_target="tpu_custom_call" | custom-call | flops 14797504512 | bytes 35094528 | tf_op jit(solution)/shard_map/pallas_call | solution.py:71
  223.9 0.3 collective-permute-start.5
  224.2 0.2 collective-permute-start
  224.4 7.1 %constant_dynamic-slice_fusion = bf16[1152,3072]{1,0:T(8,128)(2,1)} fusion(bf16[1536,6144]{1,0:T(8,128)(2,1)} %param.12, s32[]{:T(128)} %select_n.38), kind=kLoop, calls=%fused_computation.28 | loop fusion | bytes 14155780 | tf_op jit(solution)/shard_map/slice | solution.py:155
  231.5 1.1 collective-permute-start.4
  232.5 6.7 %broadcast_select_fusion.1 = (bf16[768,3072]{1,0:T(8,128)(2,1)}, bf16[768,3072]{1,0:T(8,128)(2,1)S(1)}) fusion(bf16[768,3072]{1,0:T(8,128)(2,1)} %collective-permute-done.3, bf16[768,3072]{1,0:T(8,128)(2,1)} %collective-permute-done.5, pred[]{:T(512)S(6)} %eq.41), kind=kLoop, calls=%fused_computation.8 | loop fusion | flops 4718592 | bytes 18874368 | tf_op jit(solution)/shard_map/jit(_where)/select_n | solution.py:152
  239.3 1.5 dynamic-slice-done
  240.8 2.4 pad_maximum_fusion.1
  243.2 12.9 %collective-permute-done.4 = bf16[448,1152]{1,0:T(8,128)(2,1)S(1)} collective-permute-done((bf16[448,1152]{1,0:T(8,128)(2,1)S(1)}, bf16[448,1152]{1,0:T(8,128)(2,1)S(1)}, u32[]{:S(2)}, u32[]{:S(2)}) %collective-permute-start.4) | collective-permute-done | bytes 1032224 | tf_op jit(solution)/shard_map/ppermute | solution.py:17
  256.2 1.0 copy-done.3
  257.1 11.2 %fusion.1 = f32[448,3072]{1,0:T(8,128)} fusion(bf16[768,3072]{1,0:T(8,128)(2,1)S(1)} %get-tuple-element.26, bf16[768,3072]{1,0:T(8,128)(2,1)} %get-tuple-element.25, bf16[1152,3072]{1,0:T(8,128)(2,1)} %constant_dynamic-slice_fusion, bf16[448,1152]{1,0:T(8,128)(2,1)} %copy-done.3, bf16[448,1152]{1,0:T(8,128)(2,1)S(1)} %copy-done.2), kind=kOutput, calls=%fused_computation.2 | convolution fusion | flops 6388383744 | bytes 24084480 | tf_op jit(solution)/shard_map/dot_general | solution.py:157
  268.4 1.7 slice.40.query_ref
  270.1 40.3 %all-gather.5.cloned.1.call-done.kv_ref = bf16[7168,768]{1,0:T(8,128)(2,1)} async-done(((bf16[448,768]{1,0:T(8,128)(2,1)}), bf16[7168,768]{1,0:T(8,128)(2,1)}) %all-gather.5.cloned.1.call-update) | async-done | bytes 11010064 | tf_op jit(solution)/shard_map/all_gather | solution.py:113
  310.4 14.6 %shard_map.83 = bf16[448,384]{1,0:T(8,128)(2,1)} custom-call(s32[16]{0:T(128)} %compare_select_fusion.order_ref, s32[1]{0:T(128)} %bitcast.2.count_ref, bf16[448,384]{1,0:T(8,128)(2,1)} %slice.40.query_ref, bf16[7168,768]{1,0:T(8,128)(2,1)} %all-gather.5.cloned.1.call-done.kv_ref), custom_call_target="tpu_custom_call" | custom-call | flops 4932501504 | bytes 11698176 | tf_op jit(solution)/shard_map/pallas_call | solution.py:71
  325.0 1.2 collective-permute-start.6
  326.2 0.7 iota_compare_fusion.1
  327.1 7.6 %collective-permute-done.6 = bf16[448,384]{1,0:T(8,128)(2,1)S(1)} collective-permute-done((bf16[448,384]{1,0:T(8,128)(2,1)}, bf16[448,384]{1,0:T(8,128)(2,1)S(1)}, u32[]{:S(2)}, u32[]{:S(2)}) %collective-permute-start.6) | collective-permute-done | bytes 344096 | tf_op jit(solution)/shard_map/ppermute | solution.py:17
  334.6 4.8 %fusion.8 = f32[448,3072]{1,0:T(8,128)S(1)} fusion(bf16[768,3072]{1,0:T(8,128)(2,1)} %pad_maximum_fusion.1, bf16[448,384]{1,0:T(8,128)(2,1)S(1)} %collective-permute-done.6, bf16[448,384]{1,0:T(8,128)(2,1)} %shard_map.83), kind=kOutput, calls=%fused_computation.15 | convolution fusion | flops 2115305472 | bytes 10911744 | tf_op jit(solution)/shard_map/dot_general | solution.py:167
  339.5 5.0 %add_convert_fusion = bf16[448,3072]{1,0:T(8,128)(2,1)} fusion(f32[448,3072]{1,0:T(8,128)S(1)} %bitcast.6, f32[448,3072]{1,0:T(8,128)S(1)} %fusion.8, bf16[448,3072]{1,0:T(8,128)(2,1)} %collective-permute-done, f32[3072]{0:T(1024)S(1)} %select_reduce_fusion), kind=kLoop, calls=%fused_computation.5 | loop fusion | flops 6881280 | bytes 16527360 | tf_op jit(solution)/shard_map/convert_element_type | solution.py:170
  (34 shorter events, 0.8 us)
Async XLA Ops:
  6.5 1.2 slice-start.2
  6.5 1.5 slice-start.4
  6.5 181.1 %all-gather.3.cloned.1.call-start = ((), (), s32[]{:S(2)}) async-start(), calls=%async_computation | async-start | bytes 35094528 | tf_op jit(solution)/shard_map/all_gather | solution.py:113
  6.5 4.6 %slice-start.3 = ((bf16[448,1536]{1,0:T(8,128)(2,1)}), bf16[448,384]{1,0:T(8,128)(2,1)S(1)}, s32[]{:S(2)}) async-start(bf16[448,1536]{1,0:T(8,128)(2,1)} %param.11), calls=%async_computation.6 | async-start | bytes 688128 | tf_op jit(solution)/shard_map/slice | solution.py:110
  6.5 4.6 %slice-start.5 = ((bf16[448,1536]{1,0:T(8,128)(2,1)}), bf16[448,384]{1,0:T(8,128)(2,1)S(1)}, s32[]{:S(2)}) async-start(bf16[448,1536]{1,0:T(8,128)(2,1)} %param.10), calls=%async_computation.8 | async-start | bytes 688128 | tf_op jit(solution)/shard_map/slice | solution.py:110
  9.5 300.9 %all-gather.5.cloned.1.call-start = ((), (), s32[]{:S(2)}) async-start(), calls=%async_computation.1 | async-start | bytes 11698176 | tf_op jit(solution)/shard_map/all_gather | solution.py:113
  9.6 35.3 %collective-permute-start.1 = (bf16[448,1536]{1,0:T(8,128)(2,1)}, bf16[448,1536]{1,0:T(8,128)(2,1)}, u32[]{:S(2)}, u32[]{:S(2)}) collective-permute-start(bf16[448,1536]{1,0:T(8,128)(2,1)} %param.9), channel_id=1, source_target_pairs={{0,30},{2,0},{4,2},{6,4},{8,6},{10,8},{12,10},{14,12},{16,14},{18,... | collective-permute-start | bytes 4128776 | tf_op jit(solution)/shard_map/ppermute | solution.py:17
  10.3 34.5 %collective-permute-start.2 = (s32[1]{0:T(128)}, s32[1]{0:T(128)}, u32[]{:S(2)}, u32[]{:S(2)}) collective-permute-start(s32[1]{0:T(128)} %param.14), channel_id=1, source_target_pairs={{0,30},{2,0},{4,2},{6,4},{8,6},{10,8},{12,10},{14,12},{16,14},{18,... | collective-permute-start | bytes 20 | tf_op jit(solution)/shard_map/ppermute | solution.py:17
  44.9 6.2 %copy-start.1 = (s32[16]{0:T(128)S(1)}, s32[16]{0:T(128)}, u32[]{:S(2)}) copy-start(s32[16]{0:T(128)} %param.15) | copy-start | bytes 196
  49.9 174.0 %collective-permute-start.3 = (bf16[768,3072]{1,0:T(8,128)(2,1)}, bf16[768,3072]{1,0:T(8,128)(2,1)}, u32[]{:S(2)}, u32[]{:S(2)}) collective-permute-start(bf16[768,3072]{1,0:T(8,128)(2,1)} %dynamic_slice.6), channel_id=1, source_target_pairs={{0,1},{1,0},{2,3},{3,2},{4,5},{5,4},{6,7},{7,6},{8,9},{9,8},{10,11... | collective-permute-start | bytes 14155784 | tf_op jit(solution)/shard_map/ppermute | solution.py:17
  223.9 8.7 %collective-permute-start.5 = (bf16[768,3072]{1,0:T(8,128)(2,1)}, bf16[768,3072]{1,0:T(8,128)(2,1)}, u32[]{:S(2)}, u32[]{:S(2)}) collective-permute-start(bf16[768,3072]{1,0:T(8,128)(2,1)} %collective-permute-done.3), channel_id=1, source_target_pairs={{0,2},{2,0},{4,6},{6,4},{8,10},{10,8},{12,14},{14,12},{16,18},{18,... | collective-permute-start | bytes 14155784 | tf_op jit(solution)/shard_map/ppermute | solution.py:22
  224.2 115.3 %collective-permute-start = (bf16[448,3072]{1,0:T(8,128)(2,1)}, bf16[448,3072]{1,0:T(8,128)(2,1)}, u32[]{:S(2)}, u32[]{:S(2)}) collective-permute-start(bf16[448,3072]{1,0:T(8,128)(2,1)} %param.8), channel_id=1, source_target_pairs={{0,30},{2,0},{4,2},{6,4},{8,6},{10,8},{12,10},{14,12},{16,14},{18,... | collective-permute-start | bytes 8257544 | tf_op jit(solution)/shard_map/ppermute | solution.py:17
  224.4 7.1 %copy-start.2 = (bf16[448,1152]{1,0:T(8,128)(2,1)S(1)}, bf16[448,1152]{1,0:T(8,128)(2,1)}, u32[]{:S(2)}) copy-start(bf16[448,1152]{1,0:T(8,128)(2,1)} %shard_map.82) | copy-start | bytes 3096580
  231.5 24.7 %collective-permute-start.4 = (bf16[448,1152]{1,0:T(8,128)(2,1)S(1)}, bf16[448,1152]{1,0:T(8,128)(2,1)S(1)}, u32[]{:S(2)}, u32[]{:S(2)}) collective-permute-start(bf16[448,1152]{1,0:T(8,128)(2,1)S(1)} %copy-done.2), channel_id=1, source_target_pairs={{0,1},{1,0},{2,3},{3,2},{4,5},{5,4},{6,7},{7,6},{8,9},{9,8},{10,11... | collective-permute-start | bytes 3096584 | tf_op jit(solution)/shard_map/ppermute | solution.py:17
  239.2 1.7 dynamic-slice-start
  256.2 1.0 copy-start.3
  270.1 56.8 %copy-start = (f32[64,3072]{1,0:T(8,128)S(1)}, f32[64,3072]{1,0:T(8,128)}, u32[]{:S(2)}) copy-start(f32[64,3072]{1,0:T(8,128)} %param.13) | copy-start | bytes 2359300
  325.0 9.6 %collective-permute-start.6 = (bf16[448,384]{1,0:T(8,128)(2,1)}, bf16[448,384]{1,0:T(8,128)(2,1)S(1)}, u32[]{:S(2)}, u32[]{:S(2)}) collective-permute-start(bf16[448,384]{1,0:T(8,128)(2,1)} %shard_map.83), channel_id=1, source_target_pairs={{0,1},{1,0},{2,3},{3,2},{4,5},{5,4},{6,7},{7,6},{8,9},{9,8},{10,11... | collective-permute-start | bytes 1032200 | tf_op jit(solution)/shard_map/ppermute | solution.py:17
  326.9 12.6 %slice-start = ((s8[5505024]{0:T(1024)(128)(4,1)}), s8[4194304]{0:T(1024)(128)(4,1)S(1)}, s32[]{:S(2)}) async-start(s8[5505024]{0:T(1024)(128)(4,1)} %bitcast.5), calls=%async_computation.3 | async-start | bytes 8388608
  327.0 12.4 %slice-start.1 = ((s8[5505024]{0:T(1024)(128)(4,1)}), s8[1310720]{0:T(1024)(128)(4,1)S(1)}, s32[]{:S(2)}) async-start(s8[5505024]{0:T(1024)(128)(4,1)} %bitcast.5), calls=%async_computation.4 | async-start | bytes 2621440
Sparse Core Ops, SparseCore 0:
  9.7 177.9 all-gather.2
  189.9 120.4 all-gather.4
where the time goes:
time: 355 us; the launch traced here: 351 us
  waiting for transfers between devices  226 us (64%)
  Pallas kernels  50.8 us (14%)
  local copies, waits for them, and re-layouts  20.3 us (6%)
  other arithmetic  19.2 us (5%)
  matrix products  16 us (5%)
  between operations  13.5 us (4%)
  starting transfers between devices  5.6 us (2%)
    all_gather x2, waiting for transfers between devices, gather(): return (lax.all_gather(piece, 'slot', axis=0, tiled=True), after)  172 us
    ppermute x6, waiting for transfers between devices, passed_along(): return lax.ppermute(value, axis, pairs)  53.3 us
    pallas_call x2, Pallas kernels, attend(): pl.pallas_call(attend_kernel, out_shape=jax.ShapeDtypeStruct((rows, width...  50.8 us
    dot_general x1, matrix products, per_device(): jnp.dot(shared(attended), first_weight, preferred_element_type=jnp.float32)  11.2 us
  transfers between devices with their start and end apart: 9, of which 5 were waited for; matrix products, arithmetic and copies ran while one was open for 13% of the time, Pallas kernels for 14%

commit v1 on v0

--- a/solution.py
+++ b/solution.py
@@ -22,7 +22,7 @@
     return lax.ppermute(value, "slot", [(source, source ^ 1) for source in range(count)])
 
 
-def attend_kernel(order_ref, count_ref, query_ref, kv_ref, out_ref, top, total, weighted):
+def attend_kernel(order_ref, count_ref, query_ref, kv_ref, mark_ref, out_ref, top, total, weighted):
     step = pl.program_id(0)
     width = query_ref.shape[1]
     heads = width // HD
@@ -35,14 +35,21 @@
 
     @pl.when(step < count_ref[0])
     def _():
-        for head in range(heads):
+        def score(head):
             low = head * HD
-            scores = lax.dot_general(
+            return lax.dot_general(
                 kv_ref[:, low : low + HD],
                 query_ref[:, low : low + HD],
                 (((1,), (1,)), ((), ())),
                 preferred_element_type=jnp.float32,
             )
+
+        upcoming = score(0)
+        for head in range(heads):
+            low = head * HD
+            scores = upcoming
+            if head + 1 < heads:
+                upcoming = score(head + 1)
             old_top = top[head]
             new_top = jnp.maximum(old_top, jnp.max(scores, axis=0, keepdims=True))
             expon = jnp.exp2((scores - new_top) * EXP2_SCALE)
@@ -64,7 +71,7 @@
             )
 
 
-def attend(order, count, queries, gathered, groups):
+def attend(order, count, queries, gathered, mark, groups):
     rows, width = queries.shape
     heads = width // HD
     pairs = rows * gathered.shape[0] * heads
@@ -77,6 +84,7 @@
             in_specs=[
                 pl.BlockSpec((rows, width), lambda step, order, count: (0, 0)),
                 pl.BlockSpec((rows, 2 * width), lambda step, order, count: (order[step], 0)),
+                pl.BlockSpec(mark.shape, lambda step, order, count: (0, 0)),
             ],
             out_specs=pl.BlockSpec((rows, width), lambda step, order, count: (0, 0)),
             scratch_shapes=[
@@ -91,7 +99,7 @@
             bytes_accessed=gathered.size * 2 + 4 * rows * width,
             transcendentals=pairs,
         ),
-    )(order, count, queries, gathered)
+    )(order, count, queries, gathered, mark)
 
 
 def per_device(hidden, queries, key_rows, values, out_weight, level_table, noise_level, group_live):
@@ -106,27 +114,38 @@
     heads = width // HD
     cut = (heads - max(1, heads // 4)) * HD
 
-    def gather(low, high, after=None):
-        piece = jnp.concatenate([key_rows[:, low:high], values[:, low:high]], axis=1)
-        if after is not None:
-            piece, after = lax.optimization_barrier((piece, after))
-        return lax.all_gather(piece, "slot", axis=0, tiled=True), after
+    def joined(low, high):
+        return jnp.concatenate([key_rows[:, low:high], values[:, low:high]], axis=1)
 
-    first, _ = gather(0, cut)
+    first = lax.all_gather(joined(0, cut), "slot", axis=0, tiled=True)
+    first_mark = first[:16, :HD]
     level = passed_along(noise_level, "slot", -1)
     queries = passed_along(queries, "slot", -1)
-    second, (queries, level) = gather(cut, width, (queries, level))
 
     half = width // 2
     parity = lax.rem(own_slot, 2)
     own_weight = lax.dynamic_slice(out_weight, (0, own_shard * out_width), (width, out_width))
-    halves = []
+    weights = [own_weight]
     for shift in range(1, shards):
         target = lax.rem(own_shard + shift, shards)
         sent = lax.dynamic_slice(
             out_weight, (parity * half, target * out_width), (half, out_width)
         )
-        halves.append(passed_along(sent, "tp", shift))
+        mine = passed_along(sent, "tp", shift)
+        mine, queries, level = lax.optimization_barrier((mine, queries, level))
+        other = swapped_with_pair(mine)
+        weights.append(
+            jnp.concatenate(
+                [jnp.where(parity == 0, mine, other), jnp.where(parity == 0, other, mine)], axis=0
+            )
+        )
+    first_weight = jnp.concatenate([own_weight] + [weight[:cut] for weight in weights[1:]], axis=0)
+    second_weight = jnp.concatenate([weight[cut:] for weight in weights[1:]], axis=0)
+    piece, first_mark, queries, first_weight, second_weight = lax.optimization_barrier(
+        (joined(cut, width), first_mark, queries, first_weight, second_weight)
+    )
+    second = lax.all_gather(piece, "slot", axis=0, tiled=True)
+    second_mark = second[:16, :HD]
 
     slot_ids = jnp.arange(groups, dtype=jnp.int32)
     needed = ((slot_ids < group) & (group_live == 1)) | (slot_ids == group)
@@ -138,34 +157,26 @@
     ).astype(jnp.int32)
     count = count.reshape(1)
 
-    def shared(attended):
-        others = [passed_along(attended, "tp", shift) for shift in range(1, shards)]
-        return jnp.concatenate([attended] + others, axis=1)
+    def from_others(attended):
+        return [passed_along(attended, "tp", shift) for shift in range(1, shards)]
 
-    attended = attend(order, count, queries[:, :cut], first, groups)
-    attended, queries, halves = lax.optimization_barrier((attended, queries, halves))
-    weights = [own_weight]
-    for mine in halves:
-        other = swapped_with_pair(mine)
-        weights += [
-            jnp.concatenate(
-                [jnp.where(parity == 0, mine, other), jnp.where(parity == 0, other, mine)], axis=0
-            )
-        ]
-    first_weight = jnp.concatenate([weight[:cut] for weight in weights], axis=0)
-    second_weight = jnp.concatenate([weight[cut:] for weight in weights], axis=0)
-    projected = jnp.dot(shared(attended), first_weight, preferred_element_type=jnp.float32)
     picked = jnp.arange(level_table.shape[0], dtype=jnp.int32) == level[0]
     gate_row = jnp.sum(jnp.where(picked[:, None], level_table, 0.0), axis=0)
 
-    hidden, _ = lax.optimization_barrier((hidden, second[:16, :HD]))
-    queries, projected, second_weight = lax.optimization_barrier(
-        (queries, projected, second_weight)
+    attended = attend(order, count, queries[:, :cut], first, first_mark, groups)
+    attended, queries, gate_row = lax.optimization_barrier((attended, queries, gate_row))
+    received = from_others(attended)
+    second_mark, hidden, attended = lax.optimization_barrier((second_mark, hidden, attended))
+    hidden = passed_along(hidden, "slot", -1)
+    last = attend(order, count, queries[:, cut:], second, second_mark, groups)
+    last_received = from_others(last)
+    projected = jnp.dot(
+        jnp.concatenate([attended, last] + received, axis=1),
+        first_weight,
+        preferred_element_type=jnp.float32,
     )
-    hidden = passed_along(hidden, "slot", -1)
-    attended = attend(order, count, queries[:, cut:], second, groups)
     projected = projected + jnp.dot(
-        shared(attended), second_weight, preferred_element_type=jnp.float32
+        jnp.concatenate(last_received, axis=1), second_weight, preferred_element_type=jnp.float32
     )
     return (hidden.astype(jnp.float32) + gate_row[None, :] * projected).astype(jnp.bfloat16)
 

time: 355 us -> 343 us (0.966)
  waiting for transfers between devices: 226 us -> 170 us
  other arithmetic: 19.2 us -> 44.8 us
  Pallas kernels: 50.8 us -> 66.4 us
    all_gather x2, waiting for transfers between devices: 172 us -> 61 us  [the longest x1 38.5 us: per_device(): second = lax.all_gather(piece, 'slot', axis=0, tiled=True)]
    ppermute x6, waiting for transfers between devices: 53.3 us -> 109 us  [passed_along(): return lax.ppermute(value, axis, pairs)]
    concatenate x3, other arithmetic: 4.74 us -> 31.6 us  [the longest x1 29.2 us: per_device(): jnp.concatenate([own_weight] + [weight[:cut] for weight in weights[1:]],...]
    pallas_call x2, Pallas kernels: 50.8 us -> 66.4 us  [attend(): pl.pallas_call(attend_kernel, out_shape=jax.ShapeDtypeStruct((rows, width...]
    dynamic_slice x0 -> x1, local copies, waits for them, and re-layouts: none -> 8.14 us  [per_device(): lax.dynamic_slice(out_weight, (0, own_shard * out_width), (width, out_wid...]
    convert_element_type x1 -> x0, other arithmetic: 4.98 us -> none  [per_device(): (hidden.astype(jnp.float32) + gate_row[None, :] * projected).astype(jnp.b...]
    slice x11 -> x12, local copies, waits for them, and re-layouts: 12.6 us -> 8.09 us  [the longest x1 2.26 us: per_device(): attended = attend(order, count, queries[:, :cut], first, first_mark, groups)]
  transfers between devices with their start and end apart: 9 -> 9, of which waited for: 5 -> 5; matrix products, arithmetic and copies ran while one was open for 13% -> 19% of each run, Pallas kernels for 14% -> 20%
where the time goes in v1:
time: 343 us; the launch traced here: 339 us
  waiting for transfers between devices  170 us (50%)
  Pallas kernels  66.4 us (19%)
  other arithmetic  44.8 us (13%)
  local copies, waits for them, and re-layouts  22.6 us (7%)
  matrix products  14.8 us (4%)
  between operations  13.5 us (4%)
  starting transfers between devices  6.11 us (2%)
    ppermute x6, waiting for transfers between devices, passed_along(): return lax.ppermute(value, axis, pairs)  109 us
    pallas_call x2, Pallas kernels, attend(): pl.pallas_call(attend_kernel, out_shape=jax.ShapeDtypeStruct((rows, width...  66.4 us
    all_gather x1, waiting for transfers between devices, per_device(): second = lax.all_gather(piece, 'slot', axis=0, tiled=True)  38.5 us
    concatenate x1, other arithmetic, per_device(): jnp.concatenate([own_weight] + [weight[:cut] for weight in weights[1:]],...  29.2 us
    all_gather x1, waiting for transfers between devices, per_device(): first = lax.all_gather(joined(0, cut), 'slot', axis=0, tiled=True)  22.6 us
    dot_general x1, matrix products, per_device(): jnp.dot(jnp.concatenate([attended, last] + received, axis=1), first_weigh...  13.2 us
    select_n x1, other arithmetic, per_device(): jnp.where(parity == 0, mine, other)  9.07 us
    dynamic_slice x1, local copies, waits for them, and re-layouts, per_device(): lax.dynamic_slice(out_weight, (0, own_shard * out_width), (width, out_wid...  8.14 us
  transfers between devices with their start and end apart: 9, of which 5 were waited for; matrix products, arithmetic and copies ran while one was open for 19% of the time, Pallas kernels for 20%

profile of v1, /device:TPU:25, one launch (start us, length us, event | category | flops | bytes accessed | tf_op | source)
XLA Modules:
  0.0 338.6 jit_solution(10822601153401327007)
XLA Ops:
  6.5 1.2 slice-done
  7.8 0.3 slice-done.2
  8.1 1.5 pad_maximum_fusion.1
  9.7 2.8 dynamic_slice.6
  12.5 1.3 collective-permute-start
  13.8 1.0 collective-permute-start.1
  14.7 0.6 collective-permute-start.2
  15.3 42.1 %collective-permute-done.2 = s32[1]{0:T(128)} collective-permute-done((s32[1]{0:T(128)}, s32[1]{0:T(128)}, u32[]{:S(2)}, u32[]{:S(2)}) %collective-permute-start.2) | collective-permute-done | bytes 36 | tf_op jit(solution)/shard_map/ppermute | solution.py:17
  57.4 58.0 %collective-permute-done = bf16[768,3072]{1,0:T(8,128)(2,1)} collective-permute-done((bf16[768,3072]{1,0:T(8,128)(2,1)S(1)}, bf16[768,3072]{1,0:T(8,128)(2,1)}, u32[]{:S(2)}, u32[]{:S(2)}) %collective-permute-start) | collective-permute-done | bytes 4718624 | tf_op jit(solution)/shard_map/ppermute | solution.py:17
  115.4 1.5 collective-permute-start.3
  116.9 0.9 pad_maximum_fusion.2
  117.8 8.1 %constant_dynamic-slice_fusion = bf16[1536,3072]{1,0:T(8,128)(2,1)} fusion(bf16[1536,6144]{1,0:T(8,128)(2,1)} %param.12, s32[]{:T(128)S(6)} %select_n.35), kind=kLoop, calls=%fused_computation.22 | loop fusion | bytes 18874372 | tf_op jit(solution)/shard_map/dynamic_slice | solution.py:127
  126.0 9.1 %broadcast_select_fusion.1 = (bf16[768,3072]{1,0:T(8,128)(2,1)}, bf16[768,3072]{1,0:T(8,128)(2,1)}) fusion(bf16[768,3072]{1,0:T(8,128)(2,1)} %collective-permute-done, bf16[768,3072]{1,0:T(8,128)(2,1)} %collective-permute-done.3, pred[]{:T(512)S(6)} %eq.34), kind=kLoop, calls=%fused_computation.4 | loop fusion | flops 4718592 | bytes 18874368 | tf_op jit(solution)/shard_map/jit(_where)/select_n | solution.py:139
  135.0 3.4 %slice.41 = bf16[384,3072]{1,0:T(8,128)(2,1)} slice(bf16[768,3072]{1,0:T(8,128)(2,1)} %get-tuple-element.36), slice={[384:768], [0:3072]} | slice | bytes 4718592 | tf_op jit(solution)/shard_map/slice | solution.py:143
  138.4 29.2 %fusion = bf16[2688,3072]{1,0:T(8,128)(2,1)} fusion(bf16[768,3072]{1,0:T(8,128)(2,1)S(1)} %copy-done.1, bf16[768,3072]{1,0:T(8,128)(2,1)} %get-tuple-element.35, bf16[1536,3072]{1,0:T(8,128)(2,1)S(1)} %copy-done), kind=kLoop, calls=%fused_computation.1 | loop fusion | flops 49545216 | bytes 35389440 | tf_op jit(solution)/shard_map/concatenate | solution.py:142
  167.6 22.6 %all-gather.3.cloned.1.call-done.kv_ref = bf16[7168,2304]{1,0:T(8,128)(2,1)} async-done(((bf16[448,2304]{1,0:T(8,128)(2,1)}), bf16[7168,2304]{1,0:T(8,128)(2,1)}) %all-gather.3.cloned.1.call-update) | async-done | bytes 33030160 | tf_op jit(solution)/shard_map/all_gather | solution.py:120
  190.2 1.3 slice.40.mark_ref
  191.5 0.7 convert_reduce_fusion
  192.6 1.2 compare_select_fusion.order_ref
  193.8 0.6 iota_compare_fusion.1
  194.4 1.3 select_reduce_fusion
  195.7 2.3 slice.38.query_ref
  198.0 46.2 %shard_map.82 = bf16[448,1152]{1,0:T(8,128)(2,1)} custom-call(s32[16]{0:T(128)} %compare_select_fusion.order_ref, s32[1]{0:T(128)} %bitcast.1.count_ref, bf16[448,1152]{1,0:T(8,128)(2,1)} %slice.38.query_ref, bf16[7168,2304]{1,0:T(8,128)(2,1)} %all-gather.3.cloned.1.call-done.kv_ref, bf16[16,128]{1,0:T(8,128)(2,1)} %slice.40.mark_ref), custom_call_target="tpu_custom_call" | custom-call | flops 14797504512 | bytes 35094528 | tf_op jit(solution)/shard_map/pallas_call | solution.py:78
  244.2 38.5 %all-gather.5.cloned.1.call-done.kv_ref = bf16[7168,768]{1,0:T(8,128)(2,1)} async-done(((bf16[448,768]{1,0:T(8,128)(2,1)}), bf16[7168,768]{1,0:T(8,128)(2,1)}) %all-gather.5.cloned.1.call-update) | async-done | bytes 11010064 | tf_op jit(solution)/shard_map/all_gather | solution.py:147
  282.7 1.3 slice.42.mark_ref
  284.2 1.2 collective-permute-start.5
  285.4 1.8 slice.39.query_ref
  287.1 20.2 %shard_map.83 = bf16[448,384]{1,0:T(8,128)(2,1)} custom-call(s32[16]{0:T(128)} %compare_select_fusion.order_ref, s32[1]{0:T(128)} %bitcast.1.count_ref, bf16[448,384]{1,0:T(8,128)(2,1)} %slice.39.query_ref, bf16[7168,768]{1,0:T(8,128)(2,1)} %all-gather.5.cloned.1.call-done.kv_ref, bf16[16,128]{1,0:T(8,128)(2,1)} %slice.42.mark_ref), custom_call_target="tpu_custom_call" | custom-call | flops 4932501504 | bytes 11698176 | tf_op jit(solution)/shard_map/pallas_call | solution.py:78
  307.3 0.3 collective-permute-start.6
  307.6 9.4 %collective-permute-done.6 = bf16[448,384]{1,0:T(8,128)(2,1)S(1)} collective-permute-done((bf16[448,384]{1,0:T(8,128)(2,1)}, bf16[448,384]{1,0:T(8,128)(2,1)S(1)}, u32[]{:S(2)}, u32[]{:S(2)}) %collective-permute-start.6) | collective-permute-done | bytes 344096 | tf_op jit(solution)/shard_map/ppermute | solution.py:17
  317.0 1.6 fusion.8
  318.6 13.2 %add_convert_fusion = bf16[448,3072]{1,0:T(8,128)(2,1)} fusion(f32[448,3072]{1,0:T(8,128)S(1)} %fusion.8, bf16[448,3072]{1,0:T(8,128)(2,1)} %collective-permute-done.4, bf16[2688,3072]{1,0:T(8,128)(2,1)} %fusion, f32[3072]{0:T(1024)S(1)} %select_reduce_fusion, bf16[448,1152]{1,0:T(8,128)(2,1)S(1)} %collective-permute-done.5, ...), kind=kOutput, calls=%fused_computation.2 | convolution fusion | flops 7412858880 | bytes 29945856 | tf_op jit(solution)/shard_map/dot_general | solution.py:173
  (38 shorter events, 0.8 us)
Async XLA Ops:
  6.5 1.2 slice-start
  6.5 1.5 slice-start.2
  6.5 183.7 %all-gather.3.cloned.1.call-start = ((), (), s32[]{:S(2)}) async-start(), calls=%async_computation | async-start | bytes 35094528 | tf_op jit(solution)/shard_map/all_gather | solution.py:120
  9.6 273.1 %all-gather.5.cloned.1.call-start = ((), (), s32[]{:S(2)}) async-start(), calls=%async_computation.1 | async-start | bytes 11698176 | tf_op jit(solution)/shard_map/all_gather | solution.py:147
  9.7 4.1 %copy-start.6 = (bf16[448,1536]{1,0:T(8,128)(2,1)S(1)}, bf16[448,1536]{1,0:T(8,128)(2,1)}, u32[]{:S(2)}) copy-start(bf16[448,1536]{1,0:T(8,128)(2,1)} %param.9) | copy-start | bytes 4128772
  9.7 107.2 %slice-start.1 = ((bf16[448,1536]{1,0:T(8,128)(2,1)}), bf16[448,384]{1,0:T(8,128)(2,1)S(1)}, s32[]{:S(2)}) async-start(bf16[448,1536]{1,0:T(8,128)(2,1)} %param.10), calls=%async_computation.3 | async-start | bytes 688128 | tf_op jit(solution)/shard_map/slice | solution.py:118
  9.7 107.2 %slice-start.3 = ((bf16[448,1536]{1,0:T(8,128)(2,1)}), bf16[448,384]{1,0:T(8,128)(2,1)S(1)}, s32[]{:S(2)}) async-start(bf16[448,1536]{1,0:T(8,128)(2,1)} %param.11), calls=%async_computation.5 | async-start | bytes 688128 | tf_op jit(solution)/shard_map/slice | solution.py:118
  12.5 102.8 %collective-permute-start = (bf16[768,3072]{1,0:T(8,128)(2,1)S(1)}, bf16[768,3072]{1,0:T(8,128)(2,1)}, u32[]{:S(2)}, u32[]{:S(2)}) collective-permute-start(bf16[768,3072]{1,0:T(8,128)(2,1)S(1)} %dynamic_slice.6), channel_id=1, source_target_pairs={{0,1},{1,0},{2,3},{3,2},{4,5},{5,4},{6,7},{7,6},{8,9},{9,8},{10,11... | collective-permute-start | bytes 14155784 | tf_op jit(solution)/shard_map/ppermute | solution.py:17
  13.8 43.6 %collective-permute-start.1 = (bf16[448,1536]{1,0:T(8,128)(2,1)S(1)}, bf16[448,1536]{1,0:T(8,128)(2,1)S(1)}, u32[]{:S(2)}, u32[]{:S(2)}) collective-permute-start(bf16[448,1536]{1,0:T(8,128)(2,1)S(1)} %copy-done.6), channel_id=1, source_target_pairs={{0,30},{2,0},{4,2},{6,4},{8,6},{10,8},{12,10},{14,12},{16,14},{18,... | collective-permute-start | bytes 4128776 | tf_op jit(solution)/shard_map/ppermute | solution.py:17
  14.7 42.6 %collective-permute-start.2 = (s32[1]{0:T(128)}, s32[1]{0:T(128)}, u32[]{:S(2)}, u32[]{:S(2)}) collective-permute-start(s32[1]{0:T(128)} %param.14), channel_id=1, source_target_pairs={{0,30},{2,0},{4,2},{6,4},{8,6},{10,8},{12,10},{14,12},{16,14},{18,... | collective-permute-start | bytes 20 | tf_op jit(solution)/shard_map/ppermute | solution.py:17
  57.4 58.0 %copy-start.3 = (bf16[448,1536]{1,0:T(8,128)(2,1)}, bf16[448,1536]{1,0:T(8,128)(2,1)S(1)}, u32[]{:S(2)}) copy-start(bf16[448,1536]{1,0:T(8,128)(2,1)S(1)} %collective-permute-done.1) | copy-start | bytes 4128772
  115.4 10.6 %collective-permute-start.3 = (bf16[768,3072]{1,0:T(8,128)(2,1)}, bf16[768,3072]{1,0:T(8,128)(2,1)}, u32[]{:S(2)}, u32[]{:S(2)}) collective-permute-start(bf16[768,3072]{1,0:T(8,128)(2,1)} %collective-permute-done), channel_id=1, source_target_pairs={{0,2},{2,0},{4,6},{6,4},{8,10},{10,8},{12,14},{14,12},{16,18},{18,... | collective-permute-start | bytes 14155784 | tf_op jit(solution)/shard_map/ppermute | solution.py:22
  126.0 12.5 %copy-start = (bf16[1536,3072]{1,0:T(8,128)(2,1)S(1)}, bf16[1536,3072]{1,0:T(8,128)(2,1)}, u32[]{:S(2)}) copy-start(bf16[1536,3072]{1,0:T(8,128)(2,1)} %constant_dynamic-slice_fusion) | copy-start | bytes 28311556
  135.0 3.4 %copy-start.1 = (bf16[768,3072]{1,0:T(8,128)(2,1)S(1)}, bf16[768,3072]{1,0:T(8,128)(2,1)}, u32[]{:S(2)}) copy-start(bf16[768,3072]{1,0:T(8,128)(2,1)} %get-tuple-element.36) | copy-start | bytes 14155780
  138.4 53.1 %copy-start.4 = (s32[16]{0:T(128)S(1)}, s32[16]{0:T(128)}, u32[]{:S(2)}) copy-start(s32[16]{0:T(128)} %param.15) | copy-start | bytes 196
  198.0 86.0 %copy-start.5 = (bf16[448,3072]{1,0:T(8,128)(2,1)S(1)}, bf16[448,3072]{1,0:T(8,128)(2,1)}, u32[]{:S(2)}) copy-start(bf16[448,3072]{1,0:T(8,128)(2,1)} %param.8) | copy-start | bytes 8257540
  283.9 34.7 %collective-permute-start.4 = (bf16[448,3072]{1,0:T(8,128)(2,1)S(1)}, bf16[448,3072]{1,0:T(8,128)(2,1)}, u32[]{:S(2)}, u32[]{:S(2)}) collective-permute-start(bf16[448,3072]{1,0:T(8,128)(2,1)S(1)} %copy-done.5), channel_id=1, source_target_pairs={{0,30},{2,0},{4,2},{6,4},{8,6},{10,8},{12,10},{14,12},{16,14},{18,... | collective-permute-start | bytes 8257544 | tf_op jit(solution)/shard_map/ppermute | solution.py:17
  284.2 34.4 %collective-permute-start.5 = (bf16[448,1152]{1,0:T(8,128)(2,1)}, bf16[448,1152]{1,0:T(8,128)(2,1)S(1)}, u32[]{:S(2)}, u32[]{:S(2)}) collective-permute-start(bf16[448,1152]{1,0:T(8,128)(2,1)} %shard_map.82), channel_id=1, source_target_pairs={{0,1},{1,0},{2,3},{3,2},{4,5},{5,4},{6,7},{7,6},{8,9},{9,8},{10,11... | collective-permute-start | bytes 3096584 | tf_op jit(solution)/shard_map/ppermute | solution.py:17
  287.1 29.8 %copy-start.2 = (bf16[384,3072]{1,0:T(8,128)(2,1)S(1)}, bf16[384,3072]{1,0:T(8,128)(2,1)}, u32[]{:S(2)}) copy-start(bf16[384,3072]{1,0:T(8,128)(2,1)} %slice.41) | copy-start | bytes 7077892
  307.3 11.3 %copy-start.7 = (bf16[448,1152]{1,0:T(8,128)(2,1)S(1)}, bf16[448,1152]{1,0:T(8,128)(2,1)}, u32[]{:S(2)}) copy-start(bf16[448,1152]{1,0:T(8,128)(2,1)} %shard_map.82) | copy-start | bytes 3096580
  307.3 11.3 %copy-start.8 = (bf16[448,384]{1,0:T(8,128)(2,1)S(1)}, bf16[448,384]{1,0:T(8,128)(2,1)}, u32[]{:S(2)}) copy-start(bf16[448,384]{1,0:T(8,128)(2,1)} %shard_map.83) | copy-start | bytes 1032196
  307.3 9.6 %collective-permute-start.6 = (bf16[448,384]{1,0:T(8,128)(2,1)}, bf16[448,384]{1,0:T(8,128)(2,1)S(1)}, u32[]{:S(2)}, u32[]{:S(2)}) collective-permute-start(bf16[448,384]{1,0:T(8,128)(2,1)} %shard_map.83), channel_id=1, source_target_pairs={{0,1},{1,0},{2,3},{3,2},{4,5},{5,4},{6,7},{7,6},{8,9},{9,8},{10,11... | collective-permute-start | bytes 1032200 | tf_op jit(solution)/shard_map/ppermute | solution.py:17
Sparse Core Ops, SparseCore 0:
  9.7 180.4 all-gather.2
  192.5 90.1 all-gather.4

commit v2 on v1

--- a/solution.py
+++ b/solution.py
@@ -22,7 +22,7 @@
     return lax.ppermute(value, "slot", [(source, source ^ 1) for source in range(count)])
 
 
-def attend_kernel(order_ref, count_ref, query_ref, kv_ref, mark_ref, out_ref, top, total, weighted):
+def attend_kernel(order_ref, count_ref, query_ref, kv_ref, next_ref, mark_ref, out_ref, top, total, weighted):
     step = pl.program_id(0)
     width = query_ref.shape[1]
     heads = width // HD
@@ -33,35 +33,45 @@
         total[...] = jnp.zeros(total.shape, jnp.float32)
         weighted[...] = jnp.zeros(weighted.shape, jnp.float32)
 
-    @pl.when(step < count_ref[0])
-    def _():
-        def score(head):
+    def absorb(blocks):
+        units = [(block, head) for block in blocks for head in range(heads)]
+
+        def score(unit):
+            block, head = unit
             low = head * HD
             return lax.dot_general(
-                kv_ref[:, low : low + HD],
+                block[:, low : low + HD],
                 query_ref[:, low : low + HD],
                 (((1,), (1,)), ((), ())),
                 preferred_element_type=jnp.float32,
             )
 
-        upcoming = score(0)
-        for head in range(heads):
+        upcoming = score(units[0])
+        for place, (block, head) in enumerate(units):
             low = head * HD
             scores = upcoming
-            if head + 1 < heads:
-                upcoming = score(head + 1)
+            if place + 1 < len(units):
+                upcoming = score(units[place + 1])
             old_top = top[head]
             new_top = jnp.maximum(old_top, jnp.max(scores, axis=0, keepdims=True))
             expon = jnp.exp2((scores - new_top) * EXP2_SCALE)
             shrink = jnp.exp2((old_top - new_top) * EXP2_SCALE)
             total[head] = total[head] * shrink + jnp.sum(expon, axis=0, keepdims=True)
             weighted[head] = weighted[head] * shrink + lax.dot_general(
-                kv_ref[:, width + low : width + low + HD],
+                block[:, width + low : width + low + HD],
                 expon.astype(jnp.bfloat16),
                 (((0,), (0,)), ((), ())),
                 preferred_element_type=jnp.float32,
             )
             top[head] = new_top
+
+    @pl.when(2 * step + 1 < count_ref[0])
+    def _():
+        absorb([kv_ref, next_ref])
+
+    @pl.when(2 * step + 1 == count_ref[0])
+    def _():
+        absorb([kv_ref])
 
     @pl.when(step == pl.num_programs(0) - 1)
     def _():
@@ -80,10 +90,11 @@
         out_shape=jax.ShapeDtypeStruct((rows, width), jnp.bfloat16),
         grid_spec=pltpu.PrefetchScalarGridSpec(
             num_scalar_prefetch=2,
-            grid=(groups,),
+            grid=(groups // 2,),
             in_specs=[
                 pl.BlockSpec((rows, width), lambda step, order, count: (0, 0)),
-                pl.BlockSpec((rows, 2 * width), lambda step, order, count: (order[step], 0)),
+                pl.BlockSpec((rows, 2 * width), lambda step, order, count: (order[2 * step], 0)),
+                pl.BlockSpec((rows, 2 * width), lambda step, order, count: (order[2 * step + 1], 0)),
                 pl.BlockSpec(mark.shape, lambda step, order, count: (0, 0)),
             ],
             out_specs=pl.BlockSpec((rows, width), lambda step, order, count: (0, 0)),
@@ -99,7 +110,7 @@
             bytes_accessed=gathered.size * 2 + 4 * rows * width,
             transcendentals=pairs,
         ),
-    )(order, count, queries, gathered, mark)
+    )(order, count, queries, gathered, gathered, mark)
 
 
 def per_device(hidden, queries, key_rows, values, out_weight, level_table, noise_level, group_live):
@@ -112,7 +123,7 @@
     group = lax.rem(own_slot + 1, groups)
 
     heads = width // HD
-    cut = (heads - max(1, heads // 4)) * HD
+    cut = (heads - max(1, heads // 6)) * HD
 
     def joined(low, high):
         return jnp.concatenate([key_rows[:, low:high], values[:, low:high]], axis=1)
@@ -166,7 +177,7 @@
     attended = attend(order, count, queries[:, :cut], first, first_mark, groups)
     attended, queries, gate_row = lax.optimization_barrier((attended, queries, gate_row))
     received = from_others(attended)
-    second_mark, hidden, attended = lax.optimization_barrier((second_mark, hidden, attended))
+    second_mark, hidden, received = lax.optimization_barrier((second_mark, hidden, received))
     hidden = passed_along(hidden, "slot", -1)
     last = attend(order, count, queries[:, cut:], second, second_mark, groups)
     last_received = from_others(last)
@@ -175,6 +186,7 @@
         first_weight,
         preferred_element_type=jnp.float32,
     )
+    projected, last_received = lax.optimization_barrier((projected, last_received))
     projected = projected + jnp.dot(
         jnp.concatenate(last_received, axis=1), second_weight, preferred_element_type=jnp.float32
     )

time: 343 us -> 355 us (1.035); the launches traced: 339 us -> 355 us
  waiting for transfers between devices: 170 us -> 185 us
  Pallas kernels: 66.4 us -> 72.6 us
    all_gather x1, waiting for transfers between devices: 38.5 us -> 2.51 us  [per_device(): second = lax.all_gather(piece, 'slot', axis=0, tiled=True)]
    ppermute x6, waiting for transfers between devices: 109 us -> 138 us  [passed_along(): return lax.ppermute(value, axis, pairs)]
    all_gather x1, waiting for transfers between devices: 22.6 us -> 44.8 us  [per_device(): first = lax.all_gather(joined(0, cut), 'slot', axis=0, tiled=True)]
    pallas_call x2, Pallas kernels: 66.4 us -> 72.6 us  [attend(): pl.pallas_call(attend_kernel, out_shape=jax.ShapeDtypeStruct((rows, width...]
    concatenate x1, other arithmetic: 29.2 us -> 25 us  [per_device(): jnp.concatenate([own_weight] + [weight[:cut] for weight in weights[1:]],...]
  transfers between devices with their start and end apart: 9 -> 9, of which waited for: 5 -> 6; matrix products, arithmetic and copies ran while one was open for 19% -> 20% of each run, Pallas kernels for 20% -> 16%
where the time goes in v2:
time: 355 us
  waiting for transfers between devices  185 us (52%)
  Pallas kernels  72.6 us (20%)
  other arithmetic  43.2 us (12%)
  local copies, waits for them, and re-layouts  22.1 us (6%)
  between operations  13.5 us (4%)
  matrix products  12.3 us (3%)
  starting transfers between devices  6.77 us (2%)
    ppermute x6, waiting for transfers between devices, passed_along(): return lax.ppermute(value, axis, pairs)  138 us
    pallas_call x2, Pallas kernels, attend(): pl.pallas_call(attend_kernel, out_shape=jax.ShapeDtypeStruct((rows, width...  72.6 us
    all_gather x1, waiting for transfers between devices, per_device(): first = lax.all_gather(joined(0, cut), 'slot', axis=0, tiled=True)  44.8 us
    concatenate x1, other arithmetic, per_device(): jnp.concatenate([own_weight] + [weight[:cut] for weight in weights[1:]],...  25 us
    dot_general x1, matrix products, per_device(): jnp.dot(jnp.concatenate([attended, last] + received, axis=1), first_weigh...  11.4 us
    select_n x1, other arithmetic, per_device(): jnp.where(parity == 0, mine, other)  8.85 us
    dynamic_slice x1, local copies, waits for them, and re-layouts, per_device(): lax.dynamic_slice(out_weight, (0, own_shard * out_width), (width, out_wid...  8.34 us
  transfers between devices with their start and end apart: 9, of which 6 were waited for; matrix products, arithmetic and copies ran while one was open for 20% of the time, Pallas kernels for 16%

profile of v2, /device:TPU:25, one launch (start us, length us, event | category | flops | bytes accessed | tf_op | source)
XLA Modules:
  0.0 355.5 jit_solution(1337629143945923908)
XLA Ops:
  6.5 1.3 slice-done
  8.1 1.6 pad_maximum_fusion.1
  9.8 2.8 dynamic_slice.6
  12.6 1.3 collective-permute-start
  13.9 1.0 collective-permute-start.1
  15.4 42.0 %collective-permute-done.2 = s32[1]{0:T(128)} collective-permute-done((s32[1]{0:T(128)}, s32[1]{0:T(128)}, u32[]{:S(2)}, u32[]{:S(2)}) %collective-permute-start.2) | collective-permute-done | bytes 36 | tf_op jit(solution)/shard_map/ppermute | solution.py:17
  57.5 58.0 %collective-permute-done = bf16[768,3072]{1,0:T(8,128)(2,1)} collective-permute-done((bf16[768,3072]{1,0:T(8,128)(2,1)S(1)}, bf16[768,3072]{1,0:T(8,128)(2,1)}, u32[]{:S(2)}, u32[]{:S(2)}) %collective-permute-start) | collective-permute-done | bytes 4718624 | tf_op jit(solution)/shard_map/ppermute | solution.py:17
  115.5 1.5 collective-permute-start.3
  117.0 0.8 pad_maximum_fusion.2
  117.8 8.3 %constant_dynamic-slice_fusion = bf16[1536,3072]{1,0:T(8,128)(2,1)} fusion(bf16[1536,6144]{1,0:T(8,128)(2,1)} %param.12, s32[]{:T(128)S(6)} %select_n.35), kind=kLoop, calls=%fused_computation.23 | loop fusion | bytes 18874372 | tf_op jit(solution)/shard_map/dynamic_slice | solution.py:138
  126.2 8.8 %broadcast_select_fusion.1 = (bf16[768,3072]{1,0:T(8,128)(2,1)}, bf16[768,3072]{1,0:T(8,128)(2,1)}) fusion(bf16[768,3072]{1,0:T(8,128)(2,1)} %collective-permute-done, bf16[768,3072]{1,0:T(8,128)(2,1)} %collective-permute-done.3, pred[]{:T(512)S(6)} %eq.34), kind=kLoop, calls=%fused_computation.4 | loop fusion | flops 4718592 | bytes 18874368 | tf_op jit(solution)/shard_map/jit(_where)/select_n | solution.py:150
  135.0 2.7 slice.41
  137.8 25.0 %fusion = bf16[2816,3072]{1,0:T(8,128)(2,1)} fusion(bf16[768,3072]{1,0:T(8,128)(2,1)} %get-tuple-element.40, bf16[768,3072]{1,0:T(8,128)(2,1)} %get-tuple-element.39, bf16[1536,3072]{1,0:T(8,128)(2,1)S(1)} %copy-done), kind=kLoop, calls=%fused_computation.1 | loop fusion | flops 51904512 | bytes 36175872 | tf_op jit(solution)/shard_map/concatenate | solution.py:153
  162.8 44.8 %all-gather.3.cloned.1.call-done.kv_ref.next_ref = bf16[7168,2560]{1,0:T(8,128)(2,1)} async-done(((bf16[448,2560]{1,0:T(8,128)(2,1)}), bf16[7168,2560]{1,0:T(8,128)(2,1)}) %all-gather.3.cloned.1.call-update) | async-done | bytes 36700176 | tf_op jit(solution)/shard_map/all_gather | solution.py:131
  207.6 1.3 slice.40.mark_ref
  208.9 0.6 convert_reduce_fusion
  209.9 1.1 compare_select_fusion.order_ref
  210.9 0.6 iota_compare_fusion.1
  211.6 1.3 select_reduce_fusion
  212.9 2.3 slice.38.query_ref
  215.2 57.0 %shard_map.82 = bf16[448,1280]{1,0:T(8,128)(2,1)} custom-call(s32[16]{0:T(128)} %compare_select_fusion.order_ref, s32[1]{0:T(128)} %bitcast.1.count_ref, bf16[448,1280]{1,0:T(8,128)(2,1)} %slice.38.query_ref, bf16[7168,2560]{1,0:T(8,128)(2,1)} %all-gather.3.cloned.1.call-done.kv_ref.next_ref, ...), custom_call_target="tpu_custom_call" | custom-call | flops 16441671680 | bytes 38993920 | tf_op jit(solution)/shard_map/pallas_call | solution.py:88
  272.2 1.2 collective-permute-start.4
  273.4 1.6 slice.39.query_ref
  275.0 2.5 all-gather.5.cloned.1.call-done.kv_ref.next_ref
  277.5 1.3 slice.42.mark_ref
  278.8 17.4 %collective-permute-done.4 = bf16[448,1280]{1,0:T(8,128)(2,1)} collective-permute-done((bf16[448,1280]{1,0:T(8,128)(2,1)}, bf16[448,1280]{1,0:T(8,128)(2,1)}, u32[]{:S(2)}, u32[]{:S(2)}) %collective-permute-start.4) | collective-permute-done | bytes 1146912 | tf_op jit(solution)/shard_map/ppermute | solution.py:17
  296.2 15.6 %shard_map.83 = bf16[448,256]{1,0:T(8,128)(2,1)} custom-call(s32[16]{0:T(128)} %compare_select_fusion.order_ref, s32[1]{0:T(128)} %bitcast.1.count_ref, bf16[448,256]{1,0:T(8,128)(2,1)} %slice.39.query_ref, bf16[7168,512]{1,0:T(8,128)(2,1)} %all-gather.5.cloned.1.call-done.kv_ref.next_ref, bf16[7168,512]{1,0:T(8,128)(2,1)} %all-gather.5.cloned.1.call-done.kv_ref.next_ref, ...), custom_call_target="tpu_custom_call" | custom-call | flops 3288334336 | bytes 7798784 | tf_op jit(solution)/shard_map/pallas_call | solution.py:88
  311.8 1.2 collective-permute-start.6
  313.0 11.4 %fusion.1 = f32[448,3072]{1,0:T(8,128)S(1)} fusion(bf16[2816,3072]{1,0:T(8,128)(2,1)} %fusion, bf16[448,1280]{1,0:T(8,128)(2,1)} %collective-permute-done.4, bf16[448,256]{1,0:T(8,128)(2,1)} %shard_map.83, bf16[448,1280]{1,0:T(8,128)(2,1)S(1)} %copy-done.3), kind=kOutput, calls=%fused_computation.5 | convolution fusion | flops 7758643200 | bytes 25329664 | tf_op jit(solution)/shard_map/dot_general | solution.py:184
  324.4 0.9 fusion.9
  325.3 20.1 %collective-permute-done.5 = bf16[448,3072]{1,0:T(8,128)(2,1)S(1)} collective-permute-done((bf16[448,3072]{1,0:T(8,128)(2,1)S(1)}, bf16[448,3072]{1,0:T(8,128)(2,1)S(1)}, u32[]{:S(2)}, u32[]{:S(2)}) %collective-permute-start.5) | collective-permute-done | bytes 2752544 | tf_op jit(solution)/shard_map/ppermute | solution.py:17
  345.5 3.1 add_convert_fusion
  (35 shorter events, 1.4 us)
Async XLA Ops:
  6.5 1.3 slice-start
  6.5 1.6 slice-start.2
  6.5 201.1 %all-gather.3.cloned.1.call-start = ((), (), s32[]{:S(2)}) async-start(), calls=%async_computation | async-start | bytes 38993920 | tf_op jit(solution)/shard_map/all_gather | solution.py:131
  9.7 267.8 %all-gather.5.cloned.1.call-start = ((), (), s32[]{:S(2)}) async-start(), calls=%async_computation.1 | async-start | bytes 7798784 | tf_op jit(solution)/shard_map/all_gather | solution.py:158
  9.8 4.1 %copy-start.6 = (bf16[448,1536]{1,0:T(8,128)(2,1)S(1)}, bf16[448,1536]{1,0:T(8,128)(2,1)}, u32[]{:S(2)}) copy-start(bf16[448,1536]{1,0:T(8,128)(2,1)} %param.9) | copy-start | bytes 4128772
  9.8 107.2 %slice-start.1 = ((bf16[448,1536]{1,0:T(8,128)(2,1)}), bf16[448,256]{1,0:T(8,128)(2,1)S(1)}, s32[]{:S(2)}) async-start(bf16[448,1536]{1,0:T(8,128)(2,1)} %param.10), calls=%async_computation.3 | async-start | bytes 458752 | tf_op jit(solution)/shard_map/slice | solution.py:129
  9.8 107.2 %slice-start.3 = ((bf16[448,1536]{1,0:T(8,128)(2,1)}), bf16[448,256]{1,0:T(8,128)(2,1)S(1)}, s32[]{:S(2)}) async-start(bf16[448,1536]{1,0:T(8,128)(2,1)} %param.11), calls=%async_computation.5 | async-start | bytes 458752 | tf_op jit(solution)/shard_map/slice | solution.py:129
  12.6 102.8 %collective-permute-start = (bf16[768,3072]{1,0:T(8,128)(2,1)S(1)}, bf16[768,3072]{1,0:T(8,128)(2,1)}, u32[]{:S(2)}, u32[]{:S(2)}) collective-permute-start(bf16[768,3072]{1,0:T(8,128)(2,1)S(1)} %dynamic_slice.6), channel_id=1, source_target_pairs={{0,1},{1,0},{2,3},{3,2},{4,5},{5,4},{6,7},{7,6},{8,9},{9,8},{10,11... | collective-permute-start | bytes 14155784 | tf_op jit(solution)/shard_map/ppermute | solution.py:17
  13.9 43.6 %collective-permute-start.1 = (bf16[448,1536]{1,0:T(8,128)(2,1)S(1)}, bf16[448,1536]{1,0:T(8,128)(2,1)S(1)}, u32[]{:S(2)}, u32[]{:S(2)}) collective-permute-start(bf16[448,1536]{1,0:T(8,128)(2,1)S(1)} %copy-done.6), channel_id=1, source_target_pairs={{0,30},{2,0},{4,2},{6,4},{8,6},{10,8},{12,10},{14,12},{16,14},{18,... | collective-permute-start | bytes 4128776 | tf_op jit(solution)/shard_map/ppermute | solution.py:17
  14.9 42.6 %collective-permute-start.2 = (s32[1]{0:T(128)}, s32[1]{0:T(128)}, u32[]{:S(2)}, u32[]{:S(2)}) collective-permute-start(s32[1]{0:T(128)} %param.14), channel_id=1, source_target_pairs={{0,30},{2,0},{4,2},{6,4},{8,6},{10,8},{12,10},{14,12},{16,14},{18,... | collective-permute-start | bytes 20 | tf_op jit(solution)/shard_map/ppermute | solution.py:17
  57.5 58.0 %copy-start.2 = (bf16[448,1536]{1,0:T(8,128)(2,1)}, bf16[448,1536]{1,0:T(8,128)(2,1)S(1)}, u32[]{:S(2)}) copy-start(bf16[448,1536]{1,0:T(8,128)(2,1)S(1)} %collective-permute-done.1) | copy-start | bytes 4128772
  115.5 10.7 %collective-permute-start.3 = (bf16[768,3072]{1,0:T(8,128)(2,1)}, bf16[768,3072]{1,0:T(8,128)(2,1)}, u32[]{:S(2)}, u32[]{:S(2)}) collective-permute-start(bf16[768,3072]{1,0:T(8,128)(2,1)} %collective-permute-done), channel_id=1, source_target_pairs={{0,2},{2,0},{4,6},{6,4},{8,10},{10,8},{12,14},{14,12},{16,18},{18,... | collective-permute-start | bytes 14155784 | tf_op jit(solution)/shard_map/ppermute | solution.py:22
  126.2 11.6 %copy-start = (bf16[1536,3072]{1,0:T(8,128)(2,1)S(1)}, bf16[1536,3072]{1,0:T(8,128)(2,1)}, u32[]{:S(2)}) copy-start(bf16[1536,3072]{1,0:T(8,128)(2,1)} %constant_dynamic-slice_fusion) | copy-start | bytes 28311556
  137.8 71.1 %copy-start.4 = (s32[16]{0:T(128)S(1)}, s32[16]{0:T(128)}, u32[]{:S(2)}) copy-start(s32[16]{0:T(128)} %param.15) | copy-start | bytes 196
  272.2 24.0 %collective-permute-start.4 = (bf16[448,1280]{1,0:T(8,128)(2,1)}, bf16[448,1280]{1,0:T(8,128)(2,1)}, u32[]{:S(2)}, u32[]{:S(2)}) collective-permute-start(bf16[448,1280]{1,0:T(8,128)(2,1)} %shard_map.82), channel_id=1, source_target_pairs={{0,1},{1,0},{2,3},{3,2},{4,5},{5,4},{6,7},{7,6},{8,9},{9,8},{10,11... | collective-permute-start | bytes 3440648 | tf_op jit(solution)/shard_map/ppermute | solution.py:17
  278.8 34.2 %copy-start.5 = (bf16[448,3072]{1,0:T(8,128)(2,1)S(1)}, bf16[448,3072]{1,0:T(8,128)(2,1)}, u32[]{:S(2)}) copy-start(bf16[448,3072]{1,0:T(8,128)(2,1)} %param.8) | copy-start | bytes 8257540
  278.8 34.2 %copy-start.3 = (bf16[448,1280]{1,0:T(8,128)(2,1)S(1)}, bf16[448,1280]{1,0:T(8,128)(2,1)}, u32[]{:S(2)}) copy-start(bf16[448,1280]{1,0:T(8,128)(2,1)} %shard_map.82) | copy-start | bytes 3440644
  311.8 12.6 %copy-start.1 = (bf16[256,3072]{1,0:T(8,128)(2,1)S(1)}, bf16[256,3072]{1,0:T(8,128)(2,1)}, u32[]{:S(2)}) copy-start(bf16[256,3072]{1,0:T(8,128)(2,1)} %slice.41) | copy-start | bytes 4718596
  311.8 12.6 %collective-permute-start.6 = (bf16[448,256]{1,0:T(8,128)(2,1)}, bf16[448,256]{1,0:T(8,128)(2,1)S(1)}, u32[]{:S(2)}, u32[]{:S(2)}) collective-permute-start(bf16[448,256]{1,0:T(8,128)(2,1)} %shard_map.83), channel_id=1, source_target_pairs={{0,1},{1,0},{2,3},{3,2},{4,5},{5,4},{6,7},{7,6},{8,9},{9,8},{10,11... | collective-permute-start | bytes 688136 | tf_op jit(solution)/shard_map/ppermute | solution.py:17
  313.0 32.5 %collective-permute-start.5 = (bf16[448,3072]{1,0:T(8,128)(2,1)S(1)}, bf16[448,3072]{1,0:T(8,128)(2,1)S(1)}, u32[]{:S(2)}, u32[]{:S(2)}) collective-permute-start(bf16[448,3072]{1,0:T(8,128)(2,1)S(1)} %copy-done.5), channel_id=1, source_target_pairs={{0,30},{2,0},{4,2},{6,4},{8,6},{10,8},{12,10},{14,12},{16,14},{18,... | collective-permute-start | bytes 8257544 | tf_op jit(solution)/shard_map/ppermute | solution.py:17
Sparse Core Ops, SparseCore 0:
  9.8 197.7 all-gather.2
  209.9 67.5 all-gather.4
